TPU v7x, 512 devices: a whole 4x4x16 slice. The times are simulated.
512 devices in a mesh: rows: 64 (over x, z), grp: 8 (over y, core).
Axes of the slice: x: 4, y: 4, z: 16, core: 2. Of those that a mesh axis runs over, the one named last changes fastest.
Arguments:
- sample: float32 [524288, 1024], P(('rows', 'grp')), as said below
- test_matrix: float32 [1024, 256], replicated, may hold values from -0.1875 to 0.1875
Outputs:
- basis: float32 [524288, 256], P(('rows', 'grp'))
- factor: float32 [256, 1024], replicated
Inputs may be any that keep to these rules, and one draw needn't show every extreme that they name: Every row of the sample has a positive scale and the sample has full column rank on every device.
All inputs are finite; a program needn't handle non-finite values.
Results may differ from a plain program's by a relative error of at most 0.000082.
Values sent between devices are 32-bit elements; how exact they have to be, the bound alone decides.
A program may use at most 64 MiB of HBM per device.

v0:
```python
import jax
import jax.numpy as jnp
from jax import lax
from jax.sharding import PartitionSpec as P


def partner_2(value, axis, apart):
    mask = 2**apart
    pairs = [(source, source ^ mask) for source in range(lax.axis_size(axis))]
    return lax.ppermute(value, axis, pairs)


def combine_upper(mine, partner):
    highest = lax.Precision.HIGHEST
    merged = jnp.dot(mine.T, mine, precision=highest) + jnp.dot(
        partner.T, partner, precision=highest
    )
    return jnp.linalg.cholesky(merged).T


def body(sample, test_matrix):
    highest = lax.Precision.HIGHEST
    sketch = jnp.dot(sample, test_matrix, precision=highest)
    local_gram = jnp.dot(sketch.T, sketch, precision=highest)
    group_gram = lax.psum(local_gram, "rows")
    upper = jnp.linalg.cholesky(group_gram).T
    for level in range(lax.axis_size("grp").bit_length() - 1):
        partner = partner_2(upper, "grp", level)
        upper = combine_upper(upper, partner)
    lower = upper.T
    ortho = jax.scipy.linalg.solve_triangular(lower, sketch.T, lower=True).T
    factor = lax.psum(jnp.dot(ortho.T, sample, precision=highest), ("rows", "grp"))
    total_rows = sketch.shape[0] * lax.axis_size("rows") * lax.axis_size("grp")
    basis = ortho * jnp.sqrt(jnp.float32(total_rows))
    return (basis, factor)


def solution(mesh):
    placed = (P(("rows", "grp"), None), P())
    return jax.shard_map(
        body, mesh=mesh, in_specs=placed, out_specs=(P(("rows", "grp"), None), P()), check_vma=False
    )
```

profile of v0, /device:TPU:1, one launch (start us, length us, event | category | flops | bytes accessed | tf_op | source)
XLA Modules:
  0.0 962.0 jit_solution(4966380461208958709)
XLA Ops:
  7.2 1.2 copy-done
  8.4 5.2 fusion.56
  13.6 2.5 fusion.57
  16.2 0.6 all-reduce.6.cloned.1.call-start
  16.7 257.6 %all-reduce.4.cloned.1.call-done = f32[256,256]{0,1:T(8,128)} async-done(((f32[256,256]{0,1:T(8,128)}), f32[256,256]{0,1:T(8,128)}) %all-reduce.4.cloned.1.call-update) | async-done | bytes 262160 | tf_op jit(solution)/shard_map/psum | solution.py:25
  274.3 1.1 copy.5
  275.4 1.0 fusion.6
  276.4 11.7 %cholesky.214 = f32[128,128]{1,0:T(8,128)S(1)} custom-call(f32[128,128]{1,0:T(8,128)S(1)} %cholesky.346), custom_call_target="Cholesky" | custom-call | tf_op jit(solution)/shard_map/jit(cholesky)/cholesky | solution.py:26
  288.2 9.8 %custom-call.16 = f32[1,128,128]{1,2,0:T(8,128)S(1)} custom-call(f32[1,128,128]{2,1,0:T(8,128)S(1)} %get-tuple-element.38), custom_call_target="InvertDiagBlocksLowerTriangular" | custom-call | tf_op jit(solution)/shard_map/jit(cholesky)/cholesky | solution.py:26
  298.0 0.2 constant_dynamic-update-slice_fusion.7
  298.2 0.3 convolution_subtract_fusion.1
  298.5 11.7 %cholesky.231 = f32[128,128]{1,0:T(8,128)S(1)} custom-call(f32[128,128]{1,0:T(8,128)S(1)} %convolution_subtract_fusion.1), custom_call_target="Cholesky" | custom-call | tf_op jit(solution)/shard_map/jit(cholesky)/cholesky | solution.py:26
  310.2 0.6 compare_reduce_fusion.6
  312.2 12.6 %collective-permute-start = (f32[256,256]{0,1:T(8,128)S(1)}, f32[256,256]{0,1:T(8,128)S(1)}, u32[]{:S(2)}, u32[]{:S(2)}) collective-permute-start(f32[256,256]{0,1:T(8,128)S(1)} %fusion.7), channel_id=1, source_target_pairs={{0,1},{1,0},{2,3},{3,2},{4,5},{5,4},{6,7},{7,6},{8,9},{9,8},{10,11... | collective-permute-start | bytes 786440 | tf_op jit(solution)/shard_map/ppermute | solution.py:10
  324.8 0.4 fusion.8
  325.3 0.5 collective-permute-done
  325.8 0.4 convolution_add_fusion.2
  326.2 0.1 copy.8
  326.4 11.7 %cholesky.248 = f32[128,128]{1,0:T(8,128)S(1)} custom-call(f32[128,128]{1,0:T(8,128)S(1)} %cholesky.349), custom_call_target="Cholesky" | custom-call | tf_op jit(solution)/shard_map/jit(cholesky)/cholesky | solution.py:18
  338.2 0.6 compare_reduce_fusion.5
  338.8 9.8 %custom-call.17 = f32[1,128,128]{1,2,0:T(8,128)S(1)} custom-call(f32[1,128,128]{2,1,0:T(8,128)S(1)} %get-tuple-element.34), custom_call_target="InvertDiagBlocksLowerTriangular" | custom-call | tf_op jit(solution)/shard_map/jit(cholesky)/cholesky | solution.py:18
  348.6 0.2 constant_dynamic-update-slice_fusion.5
  348.9 0.3 slice_subtract_fusion.2
  349.1 11.7 %cholesky.265 = f32[128,128]{1,0:T(8,128)S(1)} custom-call(f32[128,128]{1,0:T(8,128)S(1)} %slice_subtract_fusion.2), custom_call_target="Cholesky" | custom-call | tf_op jit(solution)/shard_map/jit(cholesky)/cholesky | solution.py:18
  360.9 0.6 compare_reduce_fusion.4
  362.9 3.3 collective-permute-start.1
  366.2 0.4 fusion.10
  366.6 5.7 collective-permute-done.1
  372.3 0.4 convolution_add_fusion.1
  372.7 0.1 copy.11
  372.9 11.7 %cholesky.282 = f32[128,128]{1,0:T(8,128)S(1)} custom-call(f32[128,128]{1,0:T(8,128)S(1)} %cholesky.352), custom_call_target="Cholesky" | custom-call | tf_op jit(solution)/shard_map/jit(cholesky)/cholesky | solution.py:18
  384.7 0.6 compare_reduce_fusion.3
  385.3 9.8 %custom-call.18 = f32[1,128,128]{1,2,0:T(8,128)S(1)} custom-call(f32[1,128,128]{2,1,0:T(8,128)S(1)} %get-tuple-element.30), custom_call_target="InvertDiagBlocksLowerTriangular" | custom-call | tf_op jit(solution)/shard_map/jit(cholesky)/cholesky | solution.py:18
  395.1 0.2 constant_dynamic-update-slice_fusion.3
  395.3 0.3 slice_subtract_fusion.1
  395.6 11.7 %cholesky.299 = f32[128,128]{1,0:T(8,128)S(1)} custom-call(f32[128,128]{1,0:T(8,128)S(1)} %slice_subtract_fusion.1), custom_call_target="Cholesky" | custom-call | tf_op jit(solution)/shard_map/jit(cholesky)/cholesky | solution.py:18
  407.3 0.6 compare_reduce_fusion.2
  409.3 5.0 collective-permute-start.2
  414.4 0.4 fusion.12
  414.8 4.5 collective-permute-done.2
  419.3 0.4 convolution_add_fusion
  419.7 0.1 copy.14
  419.9 11.7 %cholesky.316 = f32[128,128]{1,0:T(8,128)S(1)} custom-call(f32[128,128]{1,0:T(8,128)S(1)} %cholesky.355), custom_call_target="Cholesky" | custom-call | tf_op jit(solution)/shard_map/jit(cholesky)/cholesky | solution.py:18
  431.7 0.6 compare_reduce_fusion.1
  432.3 9.8 %custom-call.19 = f32[1,128,128]{1,2,0:T(8,128)S(1)} custom-call(f32[1,128,128]{2,1,0:T(8,128)S(1)} %get-tuple-element.26), custom_call_target="InvertDiagBlocksLowerTriangular" | custom-call | tf_op jit(solution)/shard_map/jit(cholesky)/cholesky | solution.py:18
  442.1 0.2 constant_dynamic-update-slice_fusion.1
  442.4 0.3 slice_subtract_fusion
  442.6 11.7 %cholesky.333 = f32[128,128]{1,0:T(8,128)S(1)} custom-call(f32[128,128]{1,0:T(8,128)S(1)} %slice_subtract_fusion), custom_call_target="Cholesky" | custom-call | tf_op jit(solution)/shard_map/jit(cholesky)/cholesky | solution.py:18
  454.4 0.7 compare_reduce_fusion
  456.5 0.1 triangular_solve.54
  456.6 4.3 while.1
  456.7 0.6 fusion.80
  457.3 1.4 bitcast_dynamic-update-slice_fusion.2
  458.8 0.6 fusion.80
  459.4 1.4 bitcast_dynamic-update-slice_fusion.2
  460.8 19.7 %custom-call.12 = f32[2,128,128]{1,2,0:T(8,128)S(1)} custom-call(f32[2,128,128]{2,1,0:T(8,128)S(1)} %get-tuple-element.10), custom_call_target="InvertDiagBlocksLowerTriangular" | custom-call | tf_op jit(solution)/shard_map/jit(_solve_triangular)/triangular_solve | solution.py:31
  480.5 0.6 fusion.1
  481.1 1.0 convolution_subtract_fusion
  482.1 0.6 fusion.23
  482.8 6.9 fusion
  489.7 1.1 multiply_bitcast_fusion
  490.8 2.5 copy.15
  493.4 459.4 %all-reduce.6.cloned.1.call-done = f32[256,1024]{1,0:T(8,128)} async-done(((f32[256,1024]{1,0:T(8,128)}), f32[256,1024]{1,0:T(8,128)}) %all-reduce.6.cloned.1.call-update) | async-done | bytes 1048592 | tf_op jit(solution)/shard_map/psum | solution.py:32
  952.7 2.3 copy.42
  (31 shorter events, 0.7 us)
Async XLA Ops:
  7.2 1.2 copy-start
  7.2 267.1 %all-reduce.4.cloned.1.call-start = ((), (), s32[]{:S(2)}) async-start(), calls=%async_computation | async-start | bytes 524288 | tf_op jit(solution)/shard_map/psum | solution.py:25
  16.2 936.5 %all-reduce.6.cloned.1.call-start = ((), (), s32[]{:S(2)}) async-start(), calls=%async_computation.1 | async-start | bytes 2097152 | tf_op jit(solution)/shard_map/psum | solution.py:32
  312.2 13.6 %collective-permute-start = (f32[256,256]{0,1:T(8,128)S(1)}, f32[256,256]{0,1:T(8,128)S(1)}, u32[]{:S(2)}, u32[]{:S(2)}) collective-permute-start(f32[256,256]{0,1:T(8,128)S(1)} %fusion.7), channel_id=1, source_target_pairs={{0,1},{1,0},{2,3},{3,2},{4,5},{5,4},{6,7},{7,6},{8,9},{9,8},{10,11... | collective-permute-start | bytes 786440 | tf_op jit(solution)/shard_map/ppermute | solution.py:10
  362.9 9.4 collective-permute-start.1
  409.3 10.0 %collective-permute-start.2 = (f32[256,256]{0,1:T(8,128)S(1)}, f32[256,256]{0,1:T(8,128)S(1)}, u32[]{:S(2)}, u32[]{:S(2)}) collective-permute-start(f32[256,256]{0,1:T(8,128)S(1)} %fusion.11), channel_id=1, source_target_pairs={{0,4},{1,5},{2,6},{3,7},{4,0},{5,1},{6,2},{7,3},{8,12},{9,13},{10,... | collective-permute-start | bytes 786440 | tf_op jit(solution)/shard_map/ppermute | solution.py:10
Sparse Core Ops, SparseCore 0:
  16.3 257.9 all-reduce.3
  489.8 462.8 all-reduce.5
where the time goes:
time: 966 us; the launch traced here: 962 us
  waiting for transfers between devices  728 us (75%)
  other arithmetic  160 us (17%)
  starting transfers between devices  21.6 us (2%)
  matrix products  21.3 us (2%)
  between operations  19.8 us (2%)
  local copies, waits for them, and re-layouts  11.7 us (1%)
    psum x1, waiting for transfers between devices, body(): lax.psum(jnp.dot(ortho.T, sample, precision=highest), ('rows', 'grp'))  459 us
    psum x1, waiting for transfers between devices, body(): group_gram = lax.psum(local_gram, 'rows')  258 us
    another operation x21, other arithmetic, combine_upper(): return jnp.linalg.cholesky(merged).T  104 us
    another operation x6, other arithmetic, body(): upper = jnp.linalg.cholesky(group_gram).T  34 us
    ppermute x3, starting transfers between devices, partner_2(): return lax.ppermute(value, axis, pairs)  21 us
    another operation x3, other arithmetic, body(): ortho = jax.scipy.linalg.solve_triangular(lower, sketch.T, lower=True).T  19.7 us
  transfers between devices with their start and end apart: 5, of which 5 were waited for; matrix products, arithmetic and copies ran while one was open for 1% of the time, Pallas kernels for 0%

commit v1 on v0

v1 whole, which is shorter than its diff:
```python
import functools

import jax
import jax.numpy as jnp
from jax import lax
from jax.experimental import pallas as pl
from jax.experimental.pallas import tpu as pltpu
from jax.sharding import PartitionSpec as P

MESH = pl.DeviceIdType.MESH
f32, bf16 = jnp.float32, jnp.bfloat16
NX, NY, NZ = 4, 4, 16
RANK, D, ROWS = 256, 1024, 1024
COLS = D // 128
PLANE = [(a, b) for a in range(NX) for b in range(NY) if a or b]


def split(v):
    hi = v.astype(bf16)
    return hi, (v - hi.astype(f32)).astype(bf16)


def mm(a, b, dims):
    def dot(u, v):
        return lax.dot_general(u, v, (dims, ((), ())), preferred_element_type=f32)

    (ah, al), (bh, bl) = a, b
    return dot(ah, bh) + (dot(ah, bl) + dot(al, bh))


def reduce_kernel(s_hbm, t_ref, sk_ref, o_ref, s_ref, sh, sl, skt, w, core_in, s0, r1, zs, rz, zt, za, out, load,
                  ssc, rsc, ss1, rs1, ssz, rsz, sgz, rgz, sg1, rg1, sgc, rgc):
    r = lax.axis_index("rows")
    g = lax.axis_index("grp")
    x, y, z, c = lax.div(r, NZ), lax.div(g, 2), lax.rem(r, NZ), lax.rem(g, 2)
    o = 1 - c

    def at(dx, dy, dz):
        return (lax.rem(x + dx, NX) * NZ + lax.rem(z + dz, NZ), lax.rem(y + dy, NY) * 2 + c)

    partner = (r, y * 2 + o)

    def copy(src, dst, ss, rs, dev):
        return pltpu.make_async_remote_copy(src_ref=src, dst_ref=dst, send_sem=ss, recv_sem=rs, device_id=dev, device_id_type=MESH)

    def rows(a, n):
        return pl.ds(pl.multiple_of(a, 8), n)

    n = ROWS // 4
    loads = [pltpu.make_async_copy(s_hbm.at[pl.ds(i * n, n)], s_ref.at[pl.ds(i * n, n)], load.at[i]) for i in range(4)]
    for k in loads:
        k.start()
    barrier = pltpu.get_barrier_semaphore()

    def greet(dev):
        pl.semaphore_signal(barrier, inc=1, device_id=dev, device_id_type=MESH)

    greet(partner)
    for dx, dy in PLANE:
        greet(at(dx, dy, 0))

    def greet_z(d, _):
        greet(at(0, 0, d))
        return 0

    lax.fori_loop(1, NZ, greet_z, 0)

    t = split(t_ref[...].T)
    for i in range(4):
        loads[i].wait()
        at_i = pl.ds(i * n, n)
        s = split(s_ref[at_i, :])
        sh[at_i, :], sl[at_i, :] = s
        skt[:, at_i] = mm(t, s, ((1,), (1,)))
    sk = split(skt[...])

    core = []
    for q in range(4):
        lanes = pl.ds(256 * q, 256)
        d = mm(sk, (sh[:, lanes], sl[:, lanes]), ((1,), (0,)))
        w[2 * q] = d[:, :128]
        w[2 * q + 1] = d[:, 128:]
        if q == 0:
            pl.semaphore_wait(barrier, 1 + len(PLANE) + NZ - 1)
        pair = pl.ds(2 * q, 2)
        k = copy(w.at[pair, rows(128 * o, 128)], core_in.at[pair], ssc.at[q], rsc.at[q], partner)
        k.start()
        core.append(k)
    for q in range(4):
        core[q].wait_recv()
        pair = pl.ds(2 * q, 2)
        s0[pair] = w[pair, rows(128 * c, 128), :] + core_in[pair]

    plane = []
    for i, (dx, dy) in enumerate(PLANE):
        q = lax.rem(x + dx, NX) * NY + lax.rem(y + dy, NY)
        k = copy(s0.at[:, rows(8 * q, 8)], r1.at[i], ss1.at[i], rs1.at[i], at(dx, dy, 0))
        k.start()
        plane.append(k)
    sk_ref[...] = skt[...].T
    own = 8 * (x * NY + y)
    for k in plane:
        k.wait_recv()
    v = s0[:, rows(own, 8), :]
    for i in range(len(PLANE)):
        v = v + r1[i]
    for j in range(COLS):
        zs[2 * j] = v[j, 0:4]
        zs[2 * j + 1] = v[j, 4:8]

    def z_copy(d):
        return copy(zs.at[lax.rem(z + d, NZ)], rz.at[d], ssz.at[d], rsz.at[d], at(0, 0, d))

    def each_z(step):
        def body(d, _):
            step(d)
            return 0

        lax.fori_loop(1, NZ, body, 0)

    each_z(lambda d: z_copy(d).start())
    each_z(lambda d: z_copy(d).wait_recv())
    v = zs[z]
    for d in range(1, NZ):
        v = v + rz[d]
    zt[...] = v
    za[z] = v

    def g_copy(d):
        return copy(zt, za.at[z], sgz.at[d], rgz.at[d], at(0, 0, d))

    each_z(lambda d: g_copy(d).start())
    each_z(lambda d: g_copy(d).wait_recv())
    mine = 128 * c + own
    for j in range(COLS):
        out[j, rows(mine, 8), :] = jnp.concatenate([za[2 * j], za[2 * j + 1]], axis=0)

    def back(i, dx, dy):
        ref = out.at[:, rows(mine, 8)]
        return copy(ref, ref, sg1.at[i], rg1.at[i], at(dx, dy, 0))

    gather = [back(i, dx, dy) for i, (dx, dy) in enumerate(PLANE)]
    for k in gather:
        k.start()
    for k in gather:
        k.wait_recv()
    ref = out.at[:, rows(128 * c, 128)]
    last = copy(ref, ref, sgc, rgc, partner)
    last.start()
    last.wait_recv()
    for k in core + plane + gather + [last]:
        k.wait_send()
    each_z(lambda d: z_copy(d).wait_send())
    each_z(lambda d: g_copy(d).wait_send())
    o_ref[...] = out[...]


def sketch_and_sum(sample, test_matrix):
    V, S = pltpu.VMEM, pltpu.SemaphoreType.DMA
    n = len(PLANE)
    return pl.pallas_call(
        reduce_kernel,
        out_shape=(jax.ShapeDtypeStruct((ROWS, RANK), f32), jax.ShapeDtypeStruct((COLS, RANK, 128), f32)),
        in_specs=[pl.BlockSpec(memory_space=pl.ANY), pl.BlockSpec(memory_space=pltpu.VMEM)],
        out_specs=(pl.BlockSpec(memory_space=pltpu.VMEM),) * 2,
        scratch_shapes=[
            V((ROWS, D), f32), V((ROWS, D), bf16), V((ROWS, D), bf16), V((RANK, ROWS), f32), V((COLS, RANK, 128), f32),
            V((COLS, 128, 128), f32), V((COLS, 128, 128), f32), V((n, COLS, 8, 128), f32), V((NZ, 4, 128), f32),
            V((NZ, 4, 128), f32), V((4, 128), f32), V((NZ, 4, 128), f32), V((COLS, RANK, 128), f32), S((4,)),
            S((4,)), S((4,)), S((n,)), S((n,)), S((NZ,)), S((NZ,)), S((NZ,)), S((NZ,)), S((n,)), S((n,)), S, S,
        ],
        compiler_params=pltpu.CompilerParams(collective_id=0, has_side_effects=True, vmem_limit_bytes=56 << 20),
    )(sample, test_matrix)


def inverse_factor(gram, x_ref, group=8):
    n = RANK
    lane = lax.broadcasted_iota(jnp.int32, (8, n), 1)
    sub = lax.broadcasted_iota(jnp.int32, (8, n), 0)
    sub1 = lax.broadcasted_iota(jnp.int32, (8, 128), 0)
    blocks = n // 8

    def wide(v):
        return jnp.concatenate([v] * (n // 128), axis=1)

    rows = [gram[8 * i : 8 * i + 8, :] for i in range(blocks)]
    for top in range(0, blocks, group):
        end = top + group
        for k in range(top, end):
            own = (lane >= 8 * k) & (lane < 8 * k + 8)
            cols = {}
            for i in range(k, end):
                cols[i] = [jnp.broadcast_to(rows[i][:, 8 * k + s : 8 * k + s + 1], (8, 128)) for s in range(8)]
                rows[i] = jnp.where(own, (lane - 8 * k == sub).astype(f32) if i == k else 0.0, rows[i])
            scale = jnp.zeros((8, 128), f32)
            for s in range(8):
                pivot = jnp.broadcast_to(cols[k][s][s : s + 1, :], (8, 128))
                inv = 1.0 / pivot
                row = jnp.broadcast_to(rows[k][s : s + 1, :], (8, n))
                heads = [jnp.broadcast_to(cols[k][u][s : s + 1, :], (8, 128)) for u in range(s + 1, 8)]
                for i in range(k, end):
                    m = cols[i][s] * inv
                    if i == k:
                        m = jnp.where(sub1 > s, m, 0.0)
                    for u in range(s + 1, 8):
                        cols[i][u] = cols[i][u] - m * heads[u - s - 1]
                    rows[i] = rows[i] - wide(m) * row
                scale = jnp.where(sub1 == s, lax.rsqrt(pivot), scale)
            rows[k] = jnp.where((lane < 8 * k + 8) | (lane >= 8 * end), rows[k] * wide(scale), 0.0)
            x_ref[8 * k : 8 * k + 8, :] = jnp.where(lane < 8 * k + 8, rows[k], 0.0)
        if end < blocks:
            v = jnp.concatenate(rows[top:end], axis=0)
            d = lax.dot_general(
                v[:, 8 * end :], v, (((0,), (0,)), ((), ())), precision=lax.Precision.HIGHEST, preferred_element_type=f32
            )
            done = (lane >= 8 * top) & (lane < 8 * end)
            for i in range(end, blocks):
                rows[i] = jnp.where(done, 0.0, rows[i]) - d[8 * (i - end) : 8 * (i - end) + 8, :]


def finish_kernel(sk_ref, w_ref, t_ref, b_ref, f_ref, x_ref, scale):
    high = lax.Precision.HIGHEST
    gram = jnp.zeros((RANK, RANK), f32)
    for j in range(0, COLS, 2):
        pair = jnp.concatenate([w_ref[j], w_ref[j + 1]], axis=1)
        gram = gram + jnp.dot(pair, t_ref[128 * j : 128 * j + 256, :], precision=high, preferred_element_type=f32)
    inverse_factor(gram, x_ref)
    x = split(x_ref[...])
    for i in range(4):
        at_i = pl.ds(256 * i, 256)
        b_ref[at_i, :] = mm(split(sk_ref[at_i, :]), x, ((1,), (1,))) * scale
        pair = jnp.concatenate([w_ref[2 * i], w_ref[2 * i + 1]], axis=1)
        f_ref[:, at_i] = mm(x, split(pair), ((1,), (0,)))


def finish(sk, total, test_matrix, scale):
    spec = pl.BlockSpec(memory_space=pltpu.VMEM)
    return pl.pallas_call(
        functools.partial(finish_kernel, scale=scale),
        out_shape=(jax.ShapeDtypeStruct((ROWS, RANK), f32), jax.ShapeDtypeStruct((RANK, D), f32)),
        in_specs=[spec] * 3,
        out_specs=(spec,) * 2,
        scratch_shapes=[pltpu.VMEM((RANK, RANK), f32)],
        compiler_params=pltpu.CompilerParams(vmem_limit_bytes=40 << 20),
    )(sk, total, test_matrix)


def body(sample, test_matrix):
    devices = lax.axis_size("rows") * lax.axis_size("grp")
    sk, total = sketch_and_sum(sample, test_matrix)
    return finish(sk, total, test_matrix, float((ROWS * devices) ** 0.5))


def solution(mesh):
    placed = (P(("rows", "grp"), None), P())
    return jax.shard_map(
        body, mesh=mesh, in_specs=placed, out_specs=(P(("rows", "grp"), None), P()), check_vma=False
    )
```

time: 966 us -> 73.7 us (0.08)
  waiting for transfers between devices: 728 us -> 0 us
  other arithmetic: 160 us -> 0 us
  Pallas kernels: 0 us -> 70.4 us
  starting transfers between devices: 21.6 us -> 0 us
  matrix products: 21.3 us -> 0 us
  between operations: 19.8 us -> 0.66 us
    psum x2 -> x0, waiting for transfers between devices: 717 us -> none  [the longest x1 459 us: body(): lax.psum(jnp.dot(ortho.T, sample, precision=highest), ('rows', 'grp'))]
    another operation x30 -> x0, other arithmetic: 157 us -> none  [the longest x21 104 us: combine_upper(): return jnp.linalg.cholesky(merged).T]
    pallas_call x0 -> x2, Pallas kernels: none -> 70.4 us  [the longest x1 58.1 us: sketch_and_sum(): pl.pallas_call(reduce_kernel, out_shape=(jax.ShapeDtypeStruct((ROWS, RANK...]
    ppermute x3 -> x0, starting transfers between devices: 21 us -> none  [partner_2(): return lax.ppermute(value, axis, pairs)]
    dot_general x9 -> x0, matrix products: 17.1 us -> none  [the longest x1 6.89 us: body(): jnp.dot(ortho.T, sample, precision=highest)]
    ppermute x3 -> x0, waiting for transfers between devices: 10.7 us -> none  [partner_2(): return lax.ppermute(value, axis, pairs)]
  transfers between devices with their start and end apart: 5 -> 0, of which waited for: 5 -> 0; matrix products, arithmetic and copies ran while one was open for 1% -> 0% of each run, Pallas kernels for 0% -> 0%
where the time goes in v1:
time: 73.7 us; the launch traced here: 73.5 us
  Pallas kernels  70.4 us (96%)
  local copies, waits for them, and re-layouts  2.45 us (3%)
    pallas_call x1, Pallas kernels, sketch_and_sum(): pl.pallas_call(reduce_kernel, out_shape=(jax.ShapeDtypeStruct((ROWS, RANK...  58.1 us
    pallas_call x1, Pallas kernels, finish(): pl.pallas_call(functools.partial(finish_kernel, scale=scale), out_shape=(...  12.3 us
    unnamed x6, local copies, waits for them, and re-layouts  2.45 us

profile of v1, /device:TPU:1, one launch (start us, length us, event | category | flops | bytes accessed | tf_op | source)
XLA Modules:
  0.0 73.5 jit_solution(1032398538946959155)
XLA Ops:
  0.6 0.0 copy-start
  0.6 58.1 %shard_map.41 = (f32[1024,256]{1,0:T(8,128)}, f32[8,256,128]{2,1,0:T(8,128)}) custom-call(f32[1024,1024]{1,0:T(8,128)} %s_hbm.1, f32[1024,256]{1,0:T(8,128)} %t_ref.3), custom_call_target="tpu_custom_call" | custom-call | tf_op jit(solution)/shard_map/pallas_call | solution.py:161
  58.8 0.0 copy-done
  58.8 0.0 copy-start.1
  58.8 1.2 %copy-done.1 = f32[1024,256]{1,0:T(8,128)S(1)} copy-done((f32[1024,256]{1,0:T(8,128)S(1)}, f32[1024,256]{1,0:T(8,128)}, u32[]{:S(2)}) %copy-start.1) | copy-done | bytes 1048600
  60.0 0.0 copy-start.2
  60.0 1.2 %copy-done.2 = f32[8,256,128]{2,1,0:T(8,128)S(1)} copy-done((f32[8,256,128]{2,1,0:T(8,128)S(1)}, f32[8,256,128]{2,1,0:T(8,128)}, u32[]{:S(2)}) %copy-start.2) | copy-done | bytes 1048600
  61.2 12.3 %shard_map.42 = (f32[1024,256]{1,0:T(8,128)}, f32[256,1024]{1,0:T(8,128)}) custom-call(f32[1024,256]{1,0:T(8,128)S(1)} %copy-done.1, f32[8,256,128]{2,1,0:T(8,128)S(1)} %copy-done.2, f32[1024,256]{1,0:T(8,128)S(1)} %copy-done), custom_call_target="tpu_custom_call" | custom-call | tf_op jit(solution)/shard_map/pallas_call | solution.py:238
Async XLA Ops:
  0.6 58.1 %copy-start = (f32[1024,256]{1,0:T(8,128)S(1)}, f32[1024,256]{1,0:T(8,128)}, u32[]{:S(2)}) copy-start(f32[1024,256]{1,0:T(8,128)} %t_ref.3) | copy-start | bytes 3145732
  58.8 1.2 %copy-start.1 = (f32[1024,256]{1,0:T(8,128)S(1)}, f32[1024,256]{1,0:T(8,128)}, u32[]{:S(2)}) copy-start(f32[1024,256]{1,0:T(8,128)} %get-tuple-element.4.sk_ref) | copy-start | bytes 3145732
  60.0 1.2 %copy-start.2 = (f32[8,256,128]{2,1,0:T(8,128)S(1)}, f32[8,256,128]{2,1,0:T(8,128)}, u32[]{:S(2)}) copy-start(f32[8,256,128]{2,1,0:T(8,128)} %get-tuple-element.5.w_ref) | copy-start | bytes 3145732

commit v2 on v1

v2 whole, which is shorter than its diff:
```python
import functools

import jax
import jax.numpy as jnp
from jax import lax
from jax.experimental import pallas as pl
from jax.experimental.pallas import tpu as pltpu
from jax.sharding import PartitionSpec as P

MESH = pl.DeviceIdType.MESH
f32, bf16 = jnp.float32, jnp.bfloat16
NX, NY, NZ = 4, 4, 16
RANK, D, ROWS = 256, 1024, 1024
COLS = D // 128
PLANE = sorted(((a, b) for a in range(NX) for b in range(NY) if a or b), key=lambda v: -min(v[0], NX - v[0]) - min(v[1], NY - v[1]))
RING = sorted(range(1, NZ), key=lambda d: -min(d, NZ - d))
PARTS = 2
PB = COLS // PARTS
PIECE = 8 * PB // NZ


def split(v):
    hi = v.astype(bf16)
    return hi, (v - hi.astype(f32)).astype(bf16)


def mm(a, b, dims):
    def dot(u, v):
        return lax.dot_general(u, v, (dims, ((), ())), preferred_element_type=f32)

    (ah, al), (bh, bl) = a, b
    return dot(ah, bh) + (dot(ah, bl) + dot(al, bh))


def reduce_kernel(s_hbm, t_hbm, sk_ref, o_ref, x_ref, s_ref, t_ref, sh, sl, skt, w, core_in, s0, r1, zs, rz, zt, za, out,
                  gl, gcore_in, gs0, gr1, gz, go, load, ssc, rsc, ssp, rsp, ssz, rsz):
    r = lax.axis_index("rows")
    g = lax.axis_index("grp")
    x, y, z, c = lax.div(r, NZ), lax.div(g, 2), lax.rem(r, NZ), lax.rem(g, 2)
    o = 1 - c

    def at(dx, dy, dz):
        return (lax.rem(x + dx, NX) * NZ + lax.rem(z + dz, NZ), lax.rem(y + dy, NY) * 2 + c)

    partner = (r, y * 2 + o)
    started = []

    def rows(a, n):
        return pl.ds(pl.multiple_of(a, 8), n)

    def send(src, dst, ss, rs, dev):
        k = pltpu.make_async_remote_copy(src_ref=src, dst_ref=dst, send_sem=ss, recv_sem=rs, device_id=dev, device_id_type=MESH)
        k.start()
        started.append(k)
        return k

    def arrive(copies):
        for k in copies:
            k.wait_recv()

    def core_send(phase, src, dst):
        return send(src, dst, ssc.at[phase], rsc.at[phase], partner)

    def plane_send(phase, src, dst):
        copies = []
        for i, (dx, dy) in enumerate(PLANE):
            q = lax.rem(x + dx, NX) * NY + lax.rem(y + dy, NY)
            copies.append(send(src(q), dst(i), ssp.at[phase, i], rsp.at[phase, i], at(dx, dy, 0)))
        return copies

    def z_send(phase, src, dst):
        return [send(src(lax.rem(z + d, NZ)), dst(d), ssz.at[phase, d], rsz.at[phase, d], at(0, 0, d)) for d in RING]

    n = ROWS // 4
    t_load = pltpu.make_async_copy(t_hbm, t_ref, load.at[4])
    t_load.start()
    loads = [pltpu.make_async_copy(s_hbm.at[pl.ds(i * n, n)], s_ref.at[pl.ds(i * n, n)], load.at[i]) for i in range(4)]
    for k in loads:
        k.start()
    barrier = pltpu.get_barrier_semaphore()

    def greet(dev):
        pl.semaphore_signal(barrier, inc=1, device_id=dev, device_id_type=MESH)

    for d in RING:
        greet(at(0, 0, d))
    for dx, dy in PLANE:
        greet(at(dx, dy, 0))
    greet(partner)

    t_load.wait()
    t = split(t_ref[...])
    gram = jnp.zeros((RANK, RANK), f32)
    for i in range(4):
        loads[i].wait()
        at_i = pl.ds(i * n, n)
        s = split(s_ref[at_i, :])
        sh[at_i, :], sl[at_i, :] = s
        part = mm(s, t, ((1,), (0,)))
        turned = part.T
        sk_ref[at_i, :] = part
        skt[:, at_i] = turned
        gram = gram + mm(split(turned), split(part), ((1,), (0,)))
    gl[0] = gram[:, :128]
    gl[1] = gram[:, 128:]
    pl.semaphore_wait(barrier, 1 + len(PLANE) + len(RING))
    mine, theirs = rows(128 * c, 128), rows(128 * o, 128)
    g_core = core_send(0, gl.at[:, theirs], gcore_in)

    sk = split(skt[...])
    w_core = []

    def multiply(q):
        lanes = pl.ds(256 * q, 256)
        d = mm(sk, (sh[:, lanes], sl[:, lanes]), ((1,), (0,)))
        w[2 * q] = d[:, :128]
        w[2 * q + 1] = d[:, 128:]
        pair = pl.ds(2 * q, 2)
        w_core.append(core_send(1 + q, w.at[pair, theirs], core_in.at[pair]))

    multiply(0)
    multiply(1)
    arrive([g_core])
    gs0[...] = gl[:, mine, :] + gcore_in[...]
    g_plane = plane_send(0, lambda q: gs0.at[:, rows(8 * q, 8)], lambda i: gr1.at[i])
    multiply(2)
    multiply(3)

    own = rows(8 * (x * NY + y), 8)
    w_plane = []
    for h in range(PARTS):
        at_h = pl.ds(PB * h, PB)
        arrive(w_core[h * 4 // PARTS : (h + 1) * 4 // PARTS])
        s0[at_h] = w[at_h, mine, :] + core_in[at_h]
        w_plane.append(plane_send(1 + h, lambda q: s0.at[at_h, rows(8 * q, 8)], lambda i: r1.at[h, i]))

    arrive(g_plane)
    v = gs0[:, own, :]
    for i in range(len(PLANE)):
        v = v + gr1[i]
    gz[z] = v
    g_z = z_send(0, lambda q: gz.at[z], lambda d: gz.at[z])

    w_z = []
    for h in range(PARTS):
        arrive(w_plane[h])
        v = s0[pl.ds(PB * h, PB), own, :]
        for i in range(len(PLANE)):
            v = v + r1[h, i]
        for j in range(PB):
            for p in range(8 // PIECE):
                zs[h, j * (8 // PIECE) + p] = v[j, p * PIECE : (p + 1) * PIECE]
        w_z.append(z_send(1 + h, lambda q: zs.at[h, q], lambda d: rz.at[h, d]))

    arrive(g_z)
    v = gz[0]
    for d in range(1, NZ):
        v = v + gz[d]
    place = rows(128 * c + 8 * (x * NY + y), 8)
    go[:, place, :] = v
    g_back = plane_send(1 + PARTS, lambda q: go.at[:, place], lambda i: go.at[:, place])

    w_all = []
    for h in range(PARTS):
        arrive(w_z[h])
        v = zs[h, z]
        for d in RING:
            v = v + rz[h, d]
        zt[h] = v
        za[h, z] = v
        w_all.append(z_send(1 + PARTS + h, lambda q: zt.at[h], lambda d: za.at[h, z]))

    arrive(g_back)
    arrive([core_send(5, go.at[:, mine], go.at[:, mine])])

    w_back = []

    def between(i):
        if i >= PARTS:
            return
        arrive(w_all[i])
        for j in range(PB):
            k = 8 // PIECE
            out[PB * i + j, place, :] = jnp.concatenate([za[i, j * k + p] for p in range(k)], axis=0)
        ref = out.at[pl.ds(PB * i, PB), place]
        w_back.append(plane_send(2 + PARTS + i, lambda q: ref, lambda d: ref))

    blocks = [jnp.concatenate([go[0, 8 * i : 8 * i + 8, :], go[1, 8 * i : 8 * i + 8, :]], axis=1) for i in range(RANK // 8)]
    inverse_factor(blocks, x_ref, between)

    last = []
    for h in range(PARTS):
        arrive(w_back[h])
        ref = out.at[pl.ds(PB * h, PB), mine]
        last.append(core_send(6 + h, ref, ref))
    arrive(last)
    for k in started:
        k.wait_send()
    o_ref[...] = out[...]


def sketch_and_sum(sample, test_matrix):
    V, S = pltpu.VMEM, pltpu.SemaphoreType.DMA
    n = len(PLANE)
    spec = pl.BlockSpec(memory_space=pltpu.VMEM)
    return pl.pallas_call(
        reduce_kernel,
        out_shape=(
            jax.ShapeDtypeStruct((ROWS, RANK), f32),
            jax.ShapeDtypeStruct((COLS, RANK, 128), f32),
            jax.ShapeDtypeStruct((RANK, RANK), f32),
        ),
        in_specs=[pl.BlockSpec(memory_space=pl.ANY)] * 2,
        out_specs=(spec,) * 3,
        scratch_shapes=[
            V((ROWS, D), f32), V((D, RANK), f32), V((ROWS, D), bf16), V((ROWS, D), bf16), V((RANK, ROWS), f32),
            V((COLS, RANK, 128), f32), V((COLS, 128, 128), f32), V((COLS, 128, 128), f32), V((PARTS, n, PB, 8, 128), f32),
            V((PARTS, NZ, PIECE, 128), f32), V((PARTS, NZ, PIECE, 128), f32), V((PARTS, PIECE, 128), f32),
            V((PARTS, NZ, PIECE, 128), f32), V((COLS, RANK, 128), f32),
            V((2, RANK, 128), f32), V((2, 128, 128), f32), V((2, 128, 128), f32), V((n, 2, 8, 128), f32),
            V((NZ, 2, 8, 128), f32), V((2, RANK, 128), f32),
            S((5,)), S((6 + PARTS,)), S((6 + PARTS,)), S((2 + 2 * PARTS, n)), S((2 + 2 * PARTS, n)),
            S((1 + 2 * PARTS, NZ)), S((1 + 2 * PARTS, NZ)),
        ],
        compiler_params=pltpu.CompilerParams(collective_id=0, has_side_effects=True, vmem_limit_bytes=60 << 20),
    )(sample, test_matrix)


def inverse_factor(rows, x_ref, between, group=8):
    n = RANK
    lane = lax.broadcasted_iota(jnp.int32, (8, n), 1)
    sub = lax.broadcasted_iota(jnp.int32, (8, n), 0)
    sub1 = lax.broadcasted_iota(jnp.int32, (8, 128), 0)
    blocks = n // 8

    def wide(v):
        return jnp.concatenate([v] * (n // 128), axis=1)

    for top in range(0, blocks, group):
        end = top + group
        for k in range(top, end):
            own = (lane >= 8 * k) & (lane < 8 * k + 8)
            cols = {}
            for i in range(k, end):
                cols[i] = [jnp.broadcast_to(rows[i][:, 8 * k + s : 8 * k + s + 1], (8, 128)) for s in range(8)]
                rows[i] = jnp.where(own, (lane - 8 * k == sub).astype(f32) if i == k else 0.0, rows[i])
            scale = jnp.zeros((8, 128), f32)
            for s in range(8):
                pivot = jnp.broadcast_to(cols[k][s][s : s + 1, :], (8, 128))
                inv = 1.0 / pivot
                row = jnp.broadcast_to(rows[k][s : s + 1, :], (8, n))
                heads = [jnp.broadcast_to(cols[k][u][s : s + 1, :], (8, 128)) for u in range(s + 1, 8)]
                for i in range(k, end):
                    m = cols[i][s] * inv
                    if i == k:
                        m = jnp.where(sub1 > s, m, 0.0)
                    for u in range(s + 1, 8):
                        cols[i][u] = cols[i][u] - m * heads[u - s - 1]
                    rows[i] = rows[i] - wide(m) * row
                scale = jnp.where(sub1 == s, lax.rsqrt(pivot), scale)
            rows[k] = jnp.where((lane < 8 * k + 8) | (lane >= 8 * end), rows[k] * wide(scale), 0.0)
            x_ref[8 * k : 8 * k + 8, :] = jnp.where(lane < 8 * k + 8, rows[k], 0.0)
        if end < blocks:
            v = jnp.concatenate(rows[top:end], axis=0)
            d = lax.dot_general(
                v[:, 8 * end :], v, (((0,), (0,)), ((), ())), precision=lax.Precision.HIGHEST, preferred_element_type=f32
            )
            done = (lane >= 8 * top) & (lane < 8 * end)
            for i in range(end, blocks):
                rows[i] = jnp.where(done, 0.0, rows[i]) - d[8 * (i - end) : 8 * (i - end) + 8, :]
        between(top // group)


def finish_kernel(sk_hbm, w_hbm, x_hbm, b_hbm, f_hbm, sk, w, x, b, f, load, store, scale):
    n = ROWS // 4

    def take(src, dst, i):
        k = pltpu.make_async_copy(src, dst, load.at[i])
        k.start()
        return k

    x_load = take(x_hbm, x, 8)
    w_load = [take(w_hbm.at[pl.ds(2 * i, 2)], w.at[pl.ds(2 * i, 2)], i) for i in range(4)]
    sk_load = [take(sk_hbm.at[pl.ds(n * i, n)], sk.at[pl.ds(n * i, n)], 4 + i) for i in range(4)]
    x_load.wait()
    inv = split(x[...])
    stores = []

    def give(src, dst, i):
        k = pltpu.make_async_copy(src, dst, store.at[i])
        k.start()
        stores.append(k)

    for i in range(4):
        lanes = pl.ds(256 * i, 256)
        w_load[i].wait()
        pair = jnp.concatenate([w[2 * i], w[2 * i + 1]], axis=1)
        f[:, lanes] = mm(inv, split(pair), ((1,), (0,)))
        give(f.at[:, lanes], f_hbm.at[:, lanes], i)
    turned = split(x[...].T)
    for i in range(4):
        at_i = pl.ds(n * i, n)
        sk_load[i].wait()
        b[at_i, :] = mm(split(sk[at_i, :]), turned, ((1,), (0,))) * scale
        give(b.at[at_i], b_hbm.at[at_i], 4 + i)
    for k in stores:
        k.wait()


def finish(sk, total, inverse, scale):
    V, S = pltpu.VMEM, pltpu.SemaphoreType.DMA
    spec = pl.BlockSpec(memory_space=pl.ANY)
    return pl.pallas_call(
        functools.partial(finish_kernel, scale=scale),
        out_shape=(jax.ShapeDtypeStruct((ROWS, RANK), f32), jax.ShapeDtypeStruct((RANK, D), f32)),
        in_specs=[spec] * 3,
        out_specs=(spec,) * 2,
        scratch_shapes=[
            V((ROWS, RANK), f32), V((COLS, RANK, 128), f32), V((RANK, RANK), f32), V((ROWS, RANK), f32), V((RANK, D), f32),
            S((9,)), S((8,)),
        ],
        compiler_params=pltpu.CompilerParams(vmem_limit_bytes=60 << 20),
    )(sk, total, inverse)


def body(sample, test_matrix):
    devices = lax.axis_size("rows") * lax.axis_size("grp")
    sk, total, inverse = sketch_and_sum(sample, test_matrix)
    return finish(sk, total, inverse, float((ROWS * devices) ** 0.5))


def solution(mesh):
    placed = (P(("rows", "grp"), None), P())
    return jax.shard_map(
        body, mesh=mesh, in_specs=placed, out_specs=(P(("rows", "grp"), None), P()), check_vma=False
    )
```

time: 73.7 us -> 64.5 us (0.88)
  Pallas kernels: 70.4 us -> 63.7 us
  local copies, waits for them, and re-layouts: 2.45 us -> 0 us
    pallas_call x1, Pallas kernels: 12.3 us -> 4.71 us  [finish(): pl.pallas_call(functools.partial(finish_kernel, scale=scale), out_shape=(...]
    unnamed x6 -> x0, local copies, waits for them, and re-layouts: 2.45 us -> none
    pallas_call x1, Pallas kernels: 58.1 us -> 59 us  [sketch_and_sum(): pl.pallas_call(reduce_kernel, out_shape=(jax.ShapeDtypeStruct((ROWS, RANK...]
where the time goes in v2:
time: 64.5 us; the launch traced here: 64.4 us
  Pallas kernels  63.7 us (99%)
    pallas_call x1, Pallas kernels, sketch_and_sum(): pl.pallas_call(reduce_kernel, out_shape=(jax.ShapeDtypeStruct((ROWS, RANK...  59 us
    pallas_call x1, Pallas kernels, finish(): pl.pallas_call(functools.partial(finish_kernel, scale=scale), out_shape=(...  4.71 us

profile of v2, /device:TPU:1, one launch (start us, length us, event | category | flops | bytes accessed | tf_op | source)
XLA Modules:
  0.0 64.4 jit_solution(4276429372850795425)
XLA Ops:
  0.6 59.0 %shard_map.41 = (f32[1024,256]{1,0:T(8,128)}, f32[8,256,128]{2,1,0:T(8,128)}, f32[256,256]{1,0:T(8,128)}) custom-call(f32[1024,1024]{1,0:T(8,128)} %s_hbm.1, f32[1024,256]{1,0:T(8,128)} %t_hbm.1), custom_call_target="tpu_custom_call" | custom-call | tf_op jit(solution)/shard_map/pallas_call | solution.py:206
  59.7 4.7 %shard_map.42 = (f32[1024,256]{1,0:T(8,128)}, f32[256,1024]{1,0:T(8,128)}) custom-call(f32[1024,256]{1,0:T(8,128)} %get-tuple-element.5.sk_hbm, f32[8,256,128]{2,1,0:T(8,128)} %get-tuple-element.6.w_hbm, f32[256,256]{1,0:T(8,128)} %get-tuple-element.7.x_hbm), custom_call_target="tpu_custom_call" | custom-call | tf_op jit(solution)/shard_map/pallas_call | solution.py:313

commit v3 on v2

--- a/solution.py
+++ b/solution.py
@@ -32,8 +32,8 @@
     return dot(ah, bh) + (dot(ah, bl) + dot(al, bh))
 
 
-def reduce_kernel(s_hbm, t_hbm, sk_ref, o_ref, x_ref, s_ref, t_ref, sh, sl, skt, w, core_in, s0, r1, zs, rz, zt, za, out,
-                  gl, gcore_in, gs0, gr1, gz, go, load, ssc, rsc, ssp, rsp, ssz, rsz):
+def reduce_kernel(s_hbm, t_hbm, b_hbm, o_hbm, x_hbm, sk_ref, x_ref, b, s_ref, t_ref, sh, sl, skt, w, core_in, s0, r1, zs, rz, zt, za, out,
+                  gl, gcore_in, gs0, gr1, gz, go, load, store, ssc, rsc, ssp, rsp, ssz, rsz, scale):
     r = lax.axis_index("rows")
     g = lax.axis_index("grp")
     x, y, z, c = lax.div(r, NZ), lax.div(g, 2), lax.rem(r, NZ), lax.rem(g, 2)
@@ -43,7 +43,7 @@
         return (lax.rem(x + dx, NX) * NZ + lax.rem(z + dz, NZ), lax.rem(y + dy, NY) * 2 + c)
 
     partner = (r, y * 2 + o)
-    started = []
+    started, kept = [], []
 
     def rows(a, n):
         return pl.ds(pl.multiple_of(a, 8), n)
@@ -71,10 +71,15 @@
     def z_send(phase, src, dst):
         return [send(src(lax.rem(z + d, NZ)), dst(d), ssz.at[phase, d], rsz.at[phase, d], at(0, 0, d)) for d in RING]
 
-    n = ROWS // 4
-    t_load = pltpu.make_async_copy(t_hbm, t_ref, load.at[4])
+    def keep(src, dst, i):
+        k = pltpu.make_async_copy(src, dst, store.at[i])
+        k.start()
+        kept.append(k)
+
+    n = ROWS // 2
+    t_load = pltpu.make_async_copy(t_hbm, t_ref, load.at[2])
     t_load.start()
-    loads = [pltpu.make_async_copy(s_hbm.at[pl.ds(i * n, n)], s_ref.at[pl.ds(i * n, n)], load.at[i]) for i in range(4)]
+    loads = [pltpu.make_async_copy(s_hbm.at[pl.ds(i * n, n)], s_ref.at[pl.ds(i * n, n)], load.at[i]) for i in range(2)]
     for k in loads:
         k.start()
     barrier = pltpu.get_barrier_semaphore()
@@ -89,50 +94,44 @@
     greet(partner)
 
     t_load.wait()
-    t = split(t_ref[...])
-    gram = jnp.zeros((RANK, RANK), f32)
-    for i in range(4):
+    t = split(t_ref[...].T)
+    for i in range(2):
         loads[i].wait()
         at_i = pl.ds(i * n, n)
         s = split(s_ref[at_i, :])
         sh[at_i, :], sl[at_i, :] = s
-        part = mm(s, t, ((1,), (0,)))
-        turned = part.T
-        sk_ref[at_i, :] = part
-        skt[:, at_i] = turned
-        gram = gram + mm(split(turned), split(part), ((1,), (0,)))
-    gl[0] = gram[:, :128]
-    gl[1] = gram[:, 128:]
-    pl.semaphore_wait(barrier, 1 + len(PLANE) + len(RING))
-    mine, theirs = rows(128 * c, 128), rows(128 * o, 128)
-    g_core = core_send(0, gl.at[:, theirs], gcore_in)
+        skt[:, at_i] = mm(t, s, ((1,), (1,)))
 
     sk = split(skt[...])
-    w_core = []
-
-    def multiply(q):
+    for q in range(4):
         lanes = pl.ds(256 * q, 256)
         d = mm(sk, (sh[:, lanes], sl[:, lanes]), ((1,), (0,)))
         w[2 * q] = d[:, :128]
         w[2 * q + 1] = d[:, 128:]
-        pair = pl.ds(2 * q, 2)
-        w_core.append(core_send(1 + q, w.at[pair, theirs], core_in.at[pair]))
-
-    multiply(0)
-    multiply(1)
+    whole = jnp.concatenate([w[j] for j in range(COLS)], axis=1)
+    gram = mm(split(whole), split(t_ref[...]), ((1,), (0,)))
+    gl[0] = gram[:, :128]
+    gl[1] = gram[:, 128:]
+
+    mine, theirs = rows(128 * c, 128), rows(128 * o, 128)
+    pl.semaphore_wait(barrier, 1 + len(PLANE) + len(RING))
+    g_core = core_send(0, gl.at[:, theirs], gcore_in)
+    w_core = []
+    for h in range(PARTS):
+        at_h = pl.ds(PB * h, PB)
+        w_core.append(core_send(1 + h, w.at[at_h, theirs], core_in.at[at_h]))
+
+    own = rows(8 * (x * NY + y), 8)
     arrive([g_core])
     gs0[...] = gl[:, mine, :] + gcore_in[...]
     g_plane = plane_send(0, lambda q: gs0.at[:, rows(8 * q, 8)], lambda i: gr1.at[i])
-    multiply(2)
-    multiply(3)
-
-    own = rows(8 * (x * NY + y), 8)
     w_plane = []
     for h in range(PARTS):
         at_h = pl.ds(PB * h, PB)
-        arrive(w_core[h * 4 // PARTS : (h + 1) * 4 // PARTS])
+        arrive(w_core[h : h + 1])
         s0[at_h] = w[at_h, mine, :] + core_in[at_h]
         w_plane.append(plane_send(1 + h, lambda q: s0.at[at_h, rows(8 * q, 8)], lambda i: r1.at[h, i]))
+    sk_ref[...] = skt[...].T
 
     arrive(g_plane)
     v = gs0[:, own, :]
@@ -171,55 +170,68 @@
         w_all.append(z_send(1 + PARTS + h, lambda q: zt.at[h], lambda d: za.at[h, z]))
 
     arrive(g_back)
-    arrive([core_send(5, go.at[:, mine], go.at[:, mine])])
+    arrive([core_send(1 + PARTS, go.at[:, mine], go.at[:, mine])])
 
     w_back = []
 
     def between(i):
-        if i >= PARTS:
+        if i != 1:
             return
-        arrive(w_all[i])
-        for j in range(PB):
-            k = 8 // PIECE
-            out[PB * i + j, place, :] = jnp.concatenate([za[i, j * k + p] for p in range(k)], axis=0)
-        ref = out.at[pl.ds(PB * i, PB), place]
-        w_back.append(plane_send(2 + PARTS + i, lambda q: ref, lambda d: ref))
+        for h in range(PARTS):
+            arrive(w_all[h])
+            for j in range(PB):
+                k = 8 // PIECE
+                out[PB * h + j, place, :] = jnp.concatenate([za[h, j * k + p] for p in range(k)], axis=0)
+            ref = out.at[pl.ds(PB * h, PB), place]
+            w_back.append(plane_send(2 + PARTS + h, lambda q: ref, lambda d: ref))
 
     blocks = [jnp.concatenate([go[0, 8 * i : 8 * i + 8, :], go[1, 8 * i : 8 * i + 8, :]], axis=1) for i in range(RANK // 8)]
     inverse_factor(blocks, x_ref, between)
 
+    keep(x_ref, x_hbm, 2 * PARTS)
+    turned = split(x_ref[...].T)
+    n = ROWS // 4
+    for i in range(4):
+        at_i = pl.ds(n * i, n)
+        b[at_i, :] = mm(split(sk_ref[at_i, :]), turned, ((1,), (0,))) * scale
+        keep(b.at[at_i], b_hbm.at[at_i], 2 * PARTS + 1 + i)
     last = []
     for h in range(PARTS):
         arrive(w_back[h])
         ref = out.at[pl.ds(PB * h, PB), mine]
-        last.append(core_send(6 + h, ref, ref))
-    arrive(last)
+        last.append(core_send(2 + PARTS + h, ref, ref))
+        keep(ref, o_hbm.at[pl.ds(PB * h, PB), mine], h)
+    for h in range(PARTS):
+        arrive(last[h : h + 1])
+        keep(out.at[pl.ds(PB * h, PB), theirs], o_hbm.at[pl.ds(PB * h, PB), theirs], PARTS + h)
     for k in started:
         k.wait_send()
-    o_ref[...] = out[...]
-
-
-def sketch_and_sum(sample, test_matrix):
+    for k in kept:
+        k.wait()
+
+
+def sketch_and_sum(sample, test_matrix, scale):
     V, S = pltpu.VMEM, pltpu.SemaphoreType.DMA
     n = len(PLANE)
-    spec = pl.BlockSpec(memory_space=pltpu.VMEM)
+    spec = pl.BlockSpec(memory_space=pl.ANY)
     return pl.pallas_call(
-        reduce_kernel,
+        functools.partial(reduce_kernel, scale=scale),
         out_shape=(
             jax.ShapeDtypeStruct((ROWS, RANK), f32),
             jax.ShapeDtypeStruct((COLS, RANK, 128), f32),
             jax.ShapeDtypeStruct((RANK, RANK), f32),
         ),
-        in_specs=[pl.BlockSpec(memory_space=pl.ANY)] * 2,
+        in_specs=[spec] * 2,
         out_specs=(spec,) * 3,
         scratch_shapes=[
+            V((ROWS, RANK), f32), V((RANK, RANK), f32), V((ROWS, RANK), f32),
             V((ROWS, D), f32), V((D, RANK), f32), V((ROWS, D), bf16), V((ROWS, D), bf16), V((RANK, ROWS), f32),
             V((COLS, RANK, 128), f32), V((COLS, 128, 128), f32), V((COLS, 128, 128), f32), V((PARTS, n, PB, 8, 128), f32),
             V((PARTS, NZ, PIECE, 128), f32), V((PARTS, NZ, PIECE, 128), f32), V((PARTS, PIECE, 128), f32),
             V((PARTS, NZ, PIECE, 128), f32), V((COLS, RANK, 128), f32),
             V((2, RANK, 128), f32), V((2, 128, 128), f32), V((2, 128, 128), f32), V((n, 2, 8, 128), f32),
             V((NZ, 2, 8, 128), f32), V((2, RANK, 128), f32),
-            S((5,)), S((6 + PARTS,)), S((6 + PARTS,)), S((2 + 2 * PARTS, n)), S((2 + 2 * PARTS, n)),
+            S((3,)), S((2 * PARTS + 5,)), S((2 + 2 * PARTS,)), S((2 + 2 * PARTS,)), S((2 + 2 * PARTS, n)), S((2 + 2 * PARTS, n)),
             S((1 + 2 * PARTS, NZ)), S((1 + 2 * PARTS, NZ)),
         ],
         compiler_params=pltpu.CompilerParams(collective_id=0, has_side_effects=True, vmem_limit_bytes=60 << 20),
@@ -271,62 +283,49 @@
         between(top // group)
 
 
-def finish_kernel(sk_hbm, w_hbm, x_hbm, b_hbm, f_hbm, sk, w, x, b, f, load, store, scale):
-    n = ROWS // 4
-
-    def take(src, dst, i):
-        k = pltpu.make_async_copy(src, dst, load.at[i])
+def finish_kernel(b_in, w_hbm, x_hbm, b_hbm, f_hbm, w, x, f, b, load, store):
+    def move(src, dst, sem):
+        k = pltpu.make_async_copy(src, dst, sem)
         k.start()
         return k
 
-    x_load = take(x_hbm, x, 8)
-    w_load = [take(w_hbm.at[pl.ds(2 * i, 2)], w.at[pl.ds(2 * i, 2)], i) for i in range(4)]
-    sk_load = [take(sk_hbm.at[pl.ds(n * i, n)], sk.at[pl.ds(n * i, n)], 4 + i) for i in range(4)]
+    n = ROWS // 2
+    x_load = move(x_hbm, x, load.at[4])
+    w_load = [move(w_hbm.at[pl.ds(2 * i, 2)], w.at[pl.ds(2 * i, 2)], load.at[i]) for i in range(4)]
+    b_load = [move(b_in.at[pl.ds(n * i, n)], b.at[pl.ds(n * i, n)], load.at[5 + i]) for i in range(2)]
     x_load.wait()
     inv = split(x[...])
     stores = []
-
-    def give(src, dst, i):
-        k = pltpu.make_async_copy(src, dst, store.at[i])
-        k.start()
-        stores.append(k)
-
     for i in range(4):
         lanes = pl.ds(256 * i, 256)
         w_load[i].wait()
         pair = jnp.concatenate([w[2 * i], w[2 * i + 1]], axis=1)
         f[:, lanes] = mm(inv, split(pair), ((1,), (0,)))
-        give(f.at[:, lanes], f_hbm.at[:, lanes], i)
-    turned = split(x[...].T)
-    for i in range(4):
-        at_i = pl.ds(n * i, n)
-        sk_load[i].wait()
-        b[at_i, :] = mm(split(sk[at_i, :]), turned, ((1,), (0,))) * scale
-        give(b.at[at_i], b_hbm.at[at_i], 4 + i)
+        stores.append(move(f.at[:, lanes], f_hbm.at[:, lanes], store.at[i]))
+    for i in range(2):
+        b_load[i].wait()
+        stores.append(move(b.at[pl.ds(n * i, n)], b_hbm.at[pl.ds(n * i, n)], store.at[4 + i]))
     for k in stores:
         k.wait()
 
 
-def finish(sk, total, inverse, scale):
+def finish(basis, total, inverse):
     V, S = pltpu.VMEM, pltpu.SemaphoreType.DMA
     spec = pl.BlockSpec(memory_space=pl.ANY)
     return pl.pallas_call(
-        functools.partial(finish_kernel, scale=scale),
+        finish_kernel,
         out_shape=(jax.ShapeDtypeStruct((ROWS, RANK), f32), jax.ShapeDtypeStruct((RANK, D), f32)),
         in_specs=[spec] * 3,
         out_specs=(spec,) * 2,
-        scratch_shapes=[
-            V((ROWS, RANK), f32), V((COLS, RANK, 128), f32), V((RANK, RANK), f32), V((ROWS, RANK), f32), V((RANK, D), f32),
-            S((9,)), S((8,)),
-        ],
+        scratch_shapes=[V((COLS, RANK, 128), f32), V((RANK, RANK), f32), V((RANK, D), f32), V((ROWS, RANK), f32), S((7,)), S((6,))],
         compiler_params=pltpu.CompilerParams(vmem_limit_bytes=60 << 20),
-    )(sk, total, inverse)
+    )(basis, total, inverse)
 
 
 def body(sample, test_matrix):
     devices = lax.axis_size("rows") * lax.axis_size("grp")
-    sk, total, inverse = sketch_and_sum(sample, test_matrix)
-    return finish(sk, total, inverse, float((ROWS * devices) ** 0.5))
+    basis, total, inverse = sketch_and_sum(sample, test_matrix, float((ROWS * devices) ** 0.5))
+    return finish(basis, total, inverse)
 
 
 def solution(mesh):

time: 64.5 us -> 61.6 us (0.955)
  Pallas kernels: 63.7 us -> 60.8 us
    pallas_call x2, Pallas kernels: 63.7 us -> 60.8 us  [the longest x1 57.2 us: sketch_and_sum(): pl.pallas_call(functools.partial(reduce_kernel, scale=scale), out_shape=(...]
where the time goes in v3:
time: 61.6 us; the launch traced here: 61.5 us
  Pallas kernels  60.8 us (99%)
  between operations  0.64 us (1%)
    pallas_call x1, Pallas kernels, sketch_and_sum(): pl.pallas_call(functools.partial(reduce_kernel, scale=scale), out_shape=(...  57.2 us
    pallas_call x1, Pallas kernels, finish(): pl.pallas_call(finish_kernel, out_shape=(jax.ShapeDtypeStruct((ROWS, RANK...  3.61 us

profile of v3, /device:TPU:1, one launch (start us, length us, event | category | flops | bytes accessed | tf_op | source)
XLA Modules:
  0.0 61.5 jit_solution(3910484660724212298)
XLA Ops:
  0.6 57.2 %shard_map.41 = (f32[1024,256]{1,0:T(8,128)}, f32[8,256,128]{2,1,0:T(8,128)}, f32[256,256]{1,0:T(8,128)}) custom-call(f32[1024,1024]{1,0:T(8,128)} %s_hbm.1, f32[1024,256]{1,0:T(8,128)} %t_hbm.1), custom_call_target="tpu_custom_call" | custom-call | tf_op jit(solution)/shard_map/pallas_call | solution.py:217
  57.8 3.6 %shard_map.42 = (f32[1024,256]{1,0:T(8,128)}, f32[256,1024]{1,0:T(8,128)}) custom-call(f32[1024,256]{1,0:T(8,128)} %get-tuple-element.5.b_in, f32[8,256,128]{2,1,0:T(8,128)} %get-tuple-element.6.w_hbm, f32[256,256]{1,0:T(8,128)} %get-tuple-element.7.x_hbm), custom_call_target="tpu_custom_call" | custom-call | tf_op jit(solution)/shard_map/pallas_call | solution.py:315

commit v4 on v3

--- a/solution.py
+++ b/solution.py
@@ -14,7 +14,7 @@
 COLS = D // 128
 PLANE = sorted(((a, b) for a in range(NX) for b in range(NY) if a or b), key=lambda v: -min(v[0], NX - v[0]) - min(v[1], NY - v[1]))
 RING = sorted(range(1, NZ), key=lambda d: -min(d, NZ - d))
-PARTS = 2
+PARTS = 1
 PB = COLS // PARTS
 PIECE = 8 * PB // NZ
 
@@ -32,8 +32,8 @@
     return dot(ah, bh) + (dot(ah, bl) + dot(al, bh))
 
 
-def reduce_kernel(s_hbm, t_hbm, b_hbm, o_hbm, x_hbm, sk_ref, x_ref, b, s_ref, t_ref, sh, sl, skt, w, core_in, s0, r1, zs, rz, zt, za, out,
-                  gl, gcore_in, gs0, gr1, gz, go, load, store, ssc, rsc, ssp, rsp, ssz, rsz, scale):
+def reduce_kernel(s_hbm, t_hbm, b, out, x_ref, sk_ref, s_ref, t_ref, sh, sl, skt, w, core_in, s0, r1, zs, rz, zt, za,
+                  gl, gcore_in, gs0, gr1, gz, go, load, ssc, rsc, ssp, rsp, ssz, rsz, scale):
     r = lax.axis_index("rows")
     g = lax.axis_index("grp")
     x, y, z, c = lax.div(r, NZ), lax.div(g, 2), lax.rem(r, NZ), lax.rem(g, 2)
@@ -43,7 +43,7 @@
         return (lax.rem(x + dx, NX) * NZ + lax.rem(z + dz, NZ), lax.rem(y + dy, NY) * 2 + c)
 
     partner = (r, y * 2 + o)
-    started, kept = [], []
+    started = []
 
     def rows(a, n):
         return pl.ds(pl.multiple_of(a, 8), n)
@@ -70,11 +70,6 @@
 
     def z_send(phase, src, dst):
         return [send(src(lax.rem(z + d, NZ)), dst(d), ssz.at[phase, d], rsz.at[phase, d], at(0, 0, d)) for d in RING]
-
-    def keep(src, dst, i):
-        k = pltpu.make_async_copy(src, dst, store.at[i])
-        k.start()
-        kept.append(k)
 
     n = ROWS // 2
     t_load = pltpu.make_async_copy(t_hbm, t_ref, load.at[2])
@@ -175,7 +170,7 @@
     w_back = []
 
     def between(i):
-        if i != 1:
+        if i != 0:
             return
         for h in range(PARTS):
             arrive(w_all[h])
@@ -188,26 +183,19 @@
     blocks = [jnp.concatenate([go[0, 8 * i : 8 * i + 8, :], go[1, 8 * i : 8 * i + 8, :]], axis=1) for i in range(RANK // 8)]
     inverse_factor(blocks, x_ref, between)
 
-    keep(x_ref, x_hbm, 2 * PARTS)
     turned = split(x_ref[...].T)
     n = ROWS // 4
     for i in range(4):
         at_i = pl.ds(n * i, n)
         b[at_i, :] = mm(split(sk_ref[at_i, :]), turned, ((1,), (0,))) * scale
-        keep(b.at[at_i], b_hbm.at[at_i], 2 * PARTS + 1 + i)
     last = []
     for h in range(PARTS):
         arrive(w_back[h])
         ref = out.at[pl.ds(PB * h, PB), mine]
         last.append(core_send(2 + PARTS + h, ref, ref))
-        keep(ref, o_hbm.at[pl.ds(PB * h, PB), mine], h)
-    for h in range(PARTS):
-        arrive(last[h : h + 1])
-        keep(out.at[pl.ds(PB * h, PB), theirs], o_hbm.at[pl.ds(PB * h, PB), theirs], PARTS + h)
+    arrive(last)
     for k in started:
         k.wait_send()
-    for k in kept:
-        k.wait()
 
 
 def sketch_and_sum(sample, test_matrix, scale):
@@ -217,24 +205,24 @@
     return pl.pallas_call(
         functools.partial(reduce_kernel, scale=scale),
         out_shape=(
-            jax.ShapeDtypeStruct((ROWS, RANK), f32),
-            jax.ShapeDtypeStruct((COLS, RANK, 128), f32),
-            jax.ShapeDtypeStruct((RANK, RANK), f32),
+            V((ROWS, RANK), f32),
+            V((COLS, RANK, 128), f32),
+            V((RANK, RANK), f32),
         ),
         in_specs=[spec] * 2,
-        out_specs=(spec,) * 3,
+        out_specs=(pl.BlockSpec(memory_space=V),) * 3,
         scratch_shapes=[
-            V((ROWS, RANK), f32), V((RANK, RANK), f32), V((ROWS, RANK), f32),
+            V((ROWS, RANK), f32),
             V((ROWS, D), f32), V((D, RANK), f32), V((ROWS, D), bf16), V((ROWS, D), bf16), V((RANK, ROWS), f32),
             V((COLS, RANK, 128), f32), V((COLS, 128, 128), f32), V((COLS, 128, 128), f32), V((PARTS, n, PB, 8, 128), f32),
             V((PARTS, NZ, PIECE, 128), f32), V((PARTS, NZ, PIECE, 128), f32), V((PARTS, PIECE, 128), f32),
-            V((PARTS, NZ, PIECE, 128), f32), V((COLS, RANK, 128), f32),
+            V((PARTS, NZ, PIECE, 128), f32),
             V((2, RANK, 128), f32), V((2, 128, 128), f32), V((2, 128, 128), f32), V((n, 2, 8, 128), f32),
             V((NZ, 2, 8, 128), f32), V((2, RANK, 128), f32),
-            S((3,)), S((2 * PARTS + 5,)), S((2 + 2 * PARTS,)), S((2 + 2 * PARTS,)), S((2 + 2 * PARTS, n)), S((2 + 2 * PARTS, n)),
+            S((3,)), S((2 + 2 * PARTS,)), S((2 + 2 * PARTS,)), S((2 + 2 * PARTS, n)), S((2 + 2 * PARTS, n)),
             S((1 + 2 * PARTS, NZ)), S((1 + 2 * PARTS, NZ)),
         ],
-        compiler_params=pltpu.CompilerParams(collective_id=0, has_side_effects=True, vmem_limit_bytes=60 << 20),
+        compiler_params=pltpu.CompilerParams(collective_id=0, has_side_effects=True, vmem_limit_bytes=61 << 20),
     )(sample, test_matrix)
 
 
@@ -283,42 +271,32 @@
         between(top // group)
 
 
-def finish_kernel(b_in, w_hbm, x_hbm, b_hbm, f_hbm, w, x, f, b, load, store):
-    def move(src, dst, sem):
-        k = pltpu.make_async_copy(src, dst, sem)
+def finish_kernel(b, w, x, b_hbm, f_hbm, f, store):
+    def give(src, dst, i):
+        k = pltpu.make_async_copy(src, dst, store.at[i])
         k.start()
         return k
 
-    n = ROWS // 2
-    x_load = move(x_hbm, x, load.at[4])
-    w_load = [move(w_hbm.at[pl.ds(2 * i, 2)], w.at[pl.ds(2 * i, 2)], load.at[i]) for i in range(4)]
-    b_load = [move(b_in.at[pl.ds(n * i, n)], b.at[pl.ds(n * i, n)], load.at[5 + i]) for i in range(2)]
-    x_load.wait()
+    stores = [give(b, b_hbm, 4)]
     inv = split(x[...])
-    stores = []
     for i in range(4):
         lanes = pl.ds(256 * i, 256)
-        w_load[i].wait()
         pair = jnp.concatenate([w[2 * i], w[2 * i + 1]], axis=1)
         f[:, lanes] = mm(inv, split(pair), ((1,), (0,)))
-        stores.append(move(f.at[:, lanes], f_hbm.at[:, lanes], store.at[i]))
-    for i in range(2):
-        b_load[i].wait()
-        stores.append(move(b.at[pl.ds(n * i, n)], b_hbm.at[pl.ds(n * i, n)], store.at[4 + i]))
+        stores.append(give(f.at[:, lanes], f_hbm.at[:, lanes], i))
     for k in stores:
         k.wait()
 
 
 def finish(basis, total, inverse):
     V, S = pltpu.VMEM, pltpu.SemaphoreType.DMA
-    spec = pl.BlockSpec(memory_space=pl.ANY)
     return pl.pallas_call(
         finish_kernel,
         out_shape=(jax.ShapeDtypeStruct((ROWS, RANK), f32), jax.ShapeDtypeStruct((RANK, D), f32)),
-        in_specs=[spec] * 3,
-        out_specs=(spec,) * 2,
-        scratch_shapes=[V((COLS, RANK, 128), f32), V((RANK, RANK), f32), V((RANK, D), f32), V((ROWS, RANK), f32), S((7,)), S((6,))],
-        compiler_params=pltpu.CompilerParams(vmem_limit_bytes=60 << 20),
+        in_specs=[pl.BlockSpec(memory_space=V)] * 3,
+        out_specs=(pl.BlockSpec(memory_space=pl.ANY),) * 2,
+        scratch_shapes=[V((RANK, D), f32), S((5,))],
+        compiler_params=pltpu.CompilerParams(vmem_limit_bytes=24 << 20),
     )(basis, total, inverse)
 
 

time: 61.6 us -> 56.9 us (0.924)
  Pallas kernels: 60.8 us -> 56.1 us
    pallas_call x1, Pallas kernels: 57.2 us -> 54.7 us  [sketch_and_sum(): pl.pallas_call(functools.partial(reduce_kernel, scale=scale), out_shape=(...]
    pallas_call x1, Pallas kernels: 3.61 us -> 1.43 us  [finish(): pl.pallas_call(finish_kernel, out_shape=(jax.ShapeDtypeStruct((ROWS, RANK...]
where the time goes in v4:
time: 56.9 us; the launch traced here: 56.8 us
  Pallas kernels  56.1 us (99%)
  between operations  0.64 us (1%)
    pallas_call x1, Pallas kernels, sketch_and_sum(): pl.pallas_call(functools.partial(reduce_kernel, scale=scale), out_shape=(...  54.7 us
    pallas_call x1, Pallas kernels, finish(): pl.pallas_call(finish_kernel, out_shape=(jax.ShapeDtypeStruct((ROWS, RANK...  1.43 us

profile of v4, /device:TPU:1, one launch (start us, length us, event | category | flops | bytes accessed | tf_op | source)
XLA Modules:
  0.0 56.8 jit_solution(13466879404836523316)
XLA Ops:
  0.6 54.7 %shard_map.41 = (f32[1024,256]{1,0:T(8,128)S(1)}, f32[8,256,128]{2,1,0:T(8,128)S(1)}, f32[256,256]{1,0:T(8,128)S(1)}) custom-call(f32[1024,1024]{1,0:T(8,128)} %s_hbm.1, f32[1024,256]{1,0:T(8,128)} %t_hbm.1), custom_call_target="tpu_custom_call" | custom-call | tf_op jit(solution)/shard_map/pallas_call | solution.py:205
  55.3 1.4 %shard_map.42 = (f32[1024,256]{1,0:T(8,128)}, f32[256,1024]{1,0:T(8,128)}) custom-call(f32[1024,256]{1,0:T(8,128)S(1)} %get-tuple-element.5.b, f32[8,256,128]{2,1,0:T(8,128)S(1)} %get-tuple-element.6.w, f32[256,256]{1,0:T(8,128)S(1)} %get-tuple-element.7.x), custom_call_target="tpu_custom_call" | custom-call | tf_op jit(solution)/shard_map/pallas_call | solution.py:293

commit v5 on v4

--- a/solution.py
+++ b/solution.py
@@ -84,12 +84,12 @@
 
     for d in RING:
         greet(at(0, 0, d))
+
+    t_load.wait()
+    t = split(t_ref[...].T)
     for dx, dy in PLANE:
         greet(at(dx, dy, 0))
     greet(partner)
-
-    t_load.wait()
-    t = split(t_ref[...].T)
     for i in range(2):
         loads[i].wait()
         at_i = pl.ds(i * n, n)
@@ -98,19 +98,19 @@
         skt[:, at_i] = mm(t, s, ((1,), (1,)))
 
     sk = split(skt[...])
+    sk_ref[...] = skt[...].T
+    gram = mm(sk, split(sk_ref[...]), ((1,), (0,)))
+    gl[0] = gram[:, :128]
+    gl[1] = gram[:, 128:]
+    mine, theirs = rows(128 * c, 128), rows(128 * o, 128)
+    pl.semaphore_wait(barrier, 1 + len(PLANE) + len(RING))
+    g_core = core_send(0, gl.at[:, theirs], gcore_in)
+
     for q in range(4):
         lanes = pl.ds(256 * q, 256)
         d = mm(sk, (sh[:, lanes], sl[:, lanes]), ((1,), (0,)))
         w[2 * q] = d[:, :128]
         w[2 * q + 1] = d[:, 128:]
-    whole = jnp.concatenate([w[j] for j in range(COLS)], axis=1)
-    gram = mm(split(whole), split(t_ref[...]), ((1,), (0,)))
-    gl[0] = gram[:, :128]
-    gl[1] = gram[:, 128:]
-
-    mine, theirs = rows(128 * c, 128), rows(128 * o, 128)
-    pl.semaphore_wait(barrier, 1 + len(PLANE) + len(RING))
-    g_core = core_send(0, gl.at[:, theirs], gcore_in)
     w_core = []
     for h in range(PARTS):
         at_h = pl.ds(PB * h, PB)
@@ -126,7 +126,6 @@
         arrive(w_core[h : h + 1])
         s0[at_h] = w[at_h, mine, :] + core_in[at_h]
         w_plane.append(plane_send(1 + h, lambda q: s0.at[at_h, rows(8 * q, 8)], lambda i: r1.at[h, i]))
-    sk_ref[...] = skt[...].T
 
     arrive(g_plane)
     v = gs0[:, own, :]
@@ -183,16 +182,16 @@
     blocks = [jnp.concatenate([go[0, 8 * i : 8 * i + 8, :], go[1, 8 * i : 8 * i + 8, :]], axis=1) for i in range(RANK // 8)]
     inverse_factor(blocks, x_ref, between)
 
+    last = []
+    for h in range(PARTS):
+        arrive(w_back[h])
+        ref = out.at[pl.ds(PB * h, PB), mine]
+        last.append(core_send(2 + PARTS + h, ref, ref))
     turned = split(x_ref[...].T)
     n = ROWS // 4
     for i in range(4):
         at_i = pl.ds(n * i, n)
         b[at_i, :] = mm(split(sk_ref[at_i, :]), turned, ((1,), (0,))) * scale
-    last = []
-    for h in range(PARTS):
-        arrive(w_back[h])
-        ref = out.at[pl.ds(PB * h, PB), mine]
-        last.append(core_send(2 + PARTS + h, ref, ref))
     arrive(last)
     for k in started:
         k.wait_send()

time: 56.9 us -> 56.8 us (level)
  no operation moved by 1% of the time
where the time goes in v5:
time: 56.8 us; the launch traced here: 56.7 us
  Pallas kernels  56 us (99%)
  between operations  0.64 us (1%)
    pallas_call x1, Pallas kernels, sketch_and_sum(): pl.pallas_call(functools.partial(reduce_kernel, scale=scale), out_shape=(...  54.6 us
    pallas_call x1, Pallas kernels, finish(): pl.pallas_call(finish_kernel, out_shape=(jax.ShapeDtypeStruct((ROWS, RANK...  1.42 us

profile of v5, /device:TPU:1, one launch (start us, length us, event | category | flops | bytes accessed | tf_op | source)
XLA Modules:
  0.0 56.7 jit_solution(13496388640093626761)
XLA Ops:
  0.6 54.6 %shard_map.41 = (f32[1024,256]{1,0:T(8,128)S(1)}, f32[8,256,128]{2,1,0:T(8,128)S(1)}, f32[256,256]{1,0:T(8,128)S(1)}) custom-call(f32[1024,1024]{1,0:T(8,128)} %s_hbm.1, f32[1024,256]{1,0:T(8,128)} %t_hbm.1), custom_call_target="tpu_custom_call" | custom-call | tf_op jit(solution)/shard_map/pallas_call | solution.py:204
  55.3 1.4 %shard_map.42 = (f32[1024,256]{1,0:T(8,128)}, f32[256,1024]{1,0:T(8,128)}) custom-call(f32[1024,256]{1,0:T(8,128)S(1)} %get-tuple-element.5.b, f32[8,256,128]{2,1,0:T(8,128)S(1)} %get-tuple-element.6.w, f32[256,256]{1,0:T(8,128)S(1)} %get-tuple-element.7.x), custom_call_target="tpu_custom_call" | custom-call | tf_op jit(solution)/shard_map/pallas_call | solution.py:292
